TPU v7x, 32 devices: a whole 2x2x4 slice. The times are simulated.
32 devices in a mesh: blk: 16 (over z, y, x), grp: 2 (over core).
Axes of the slice: x: 2, y: 2, z: 4, core: 2. Of those that a mesh axis runs over, the one named last changes fastest.
Arguments:
- query_tokens: bfloat16 [1024, 32, 768], P(('blk', 'grp')), may hold values from -6 to 6
- passage_tokens: bfloat16 [64, 512, 768], P(('blk', 'grp')), may hold values from -6 to 6
- lengths: int32 [64, 4], P(('blk', 'grp')), may hold values from 1 to 256, 512 in all within a row
- labels: int32 [1024], P(('blk', 'grp')), may hold values from 0 to 255
- attn_in: bfloat16 [2, 768, 2304], replicated, may hold values from -0.21875 to 0.21875
- attn_out: bfloat16 [2, 768, 768], replicated, may hold values from -1.75 to 1.75
- ffn_in: bfloat16 [2, 768, 3072], replicated, may hold values from -0.21875 to 0.21875
- ffn_out: bfloat16 [2, 3072, 768], replicated, may hold values from -0.109375 to 0.109375
- gains: float32 [2, 2, 768], replicated, may hold values from 0.5 to 1.5
- biases: float32 [2, 6, 768], replicated, may hold values from -1.2 to 1.2
- ffn_bias: float32 [2, 3072], replicated, may hold values from -1.2 to 1.2
Outputs:
- query_losses: float32 [1024], P(('blk', 'grp'))
- query_out: bfloat16 [1024, 32, 768], P(('blk', 'grp'))
- passage_out: bfloat16 [64, 512, 768], P(('blk', 'grp'))
- query_grad: float32 [1024, 32, 768], P(('blk', 'grp'))
- passage_grad: float32 [64, 512, 768], P(('blk', 'grp'))
- grad_attn_in: float32 [2, 768, 2304], P(None, 'blk')
- grad_attn_out: float32 [2, 768, 768], P(None, 'blk')
- grad_ffn_in: float32 [2, 768, 3072], P(None, 'blk')
- grad_ffn_out: float32 [2, 3072, 768], P(None, 'blk')
- grad_gains: float32 [2, 2, 768], P(None, None, 'blk')
- grad_biases: float32 [2, 6, 768], P(None, None, 'blk')
- grad_ffn_bias: float32 [2, 3072], P(None, 'blk')
Inputs may be any that keep to these rules, and one draw needn't show every extreme that they name: In each row the lengths sum to 512, and the longest is exactly 256.
All inputs are finite; a program needn't handle non-finite values.
Results may differ from a plain program's by a relative error of at most 0.024.
Values may be sent and summed in bfloat16 or wider, within the bound.
A program may use at most 256 MiB of HBM per device.

v0:
```python
import jax
import jax.numpy as jnp
from jax import lax
from jax.sharding import PartitionSpec as P

HEAD_DIM = 64


EPSILON = 1e-05
SCORE_SCALE = 0.08
KEY_SCALE = 0.125


def layer_norm(residual, gain_vec, shift_vec):
    centre = residual - jnp.mean(residual, -1, keepdims=True)
    inverse = lax.rsqrt(jnp.mean(centre * centre, -1, keepdims=True) + EPSILON)
    return centre * inverse * gain_vec + shift_vec


def norm_back(residual, gain_vec, upstream):
    centre = residual - jnp.mean(residual, -1, keepdims=True)
    inverse = lax.rsqrt(jnp.mean(centre * centre, -1, keepdims=True) + EPSILON)
    normed = centre * inverse
    scaled = upstream * gain_vec
    grad_res = inverse * (
        scaled
        - jnp.mean(scaled, -1, keepdims=True)
        - normed * jnp.mean(scaled * normed, -1, keepdims=True)
    )
    return (grad_res, jnp.sum(upstream * normed, 0), jnp.sum(upstream, 0))


def cls_index(starts, seq_len):
    return (jnp.arange(starts.shape[0], dtype=jnp.int32)[:, None] * seq_len + starts).reshape(-1)


def forward(tokens, segment, starts, params):
    attn_in, attn_out, ffn_in, ffn_out, gains, biases, ffn_bias = params
    batch_size, seq_len, feature = tokens.shape
    head_count = feature // HEAD_DIM
    flat_tokens = tokens.reshape(batch_size * seq_len, feature)
    zeros_vec = jnp.zeros_like(biases[0])
    joined = jnp.dot(flat_tokens, attn_in, preferred_element_type=jnp.float32) + jnp.concatenate(
        [biases[0], zeros_vec, biases[1]]
    )
    joined = joined.astype(jnp.bfloat16)
    shaped = joined.reshape(batch_size, seq_len, 3, head_count, HEAD_DIM)
    scores = (
        jnp.einsum(
            "bqhd,bkhd->bhqk", shaped[:, :, 0], shaped[:, :, 1], preferred_element_type=jnp.float32
        )
        * KEY_SCALE
    )
    same_seg = segment[:, :, None] == segment[:, None, :]
    scores = jnp.where(same_seg[:, None], scores, -1000000000.0)
    attention = jax.nn.softmax(scores, -1).astype(jnp.bfloat16)
    mixed = jnp.einsum(
        "bhqk,bkhd->bqhd", attention, shaped[:, :, 2], preferred_element_type=jnp.float32
    )
    mixed = mixed.reshape(batch_size * seq_len, feature).astype(jnp.bfloat16)
    first_sum = flat_tokens.astype(jnp.float32) + (
        jnp.dot(mixed, attn_out, preferred_element_type=jnp.float32) + biases[2]
    )
    hidden = layer_norm(first_sum, gains[0], biases[3]).astype(jnp.bfloat16)
    inner = jnp.dot(hidden, ffn_in, preferred_element_type=jnp.float32) + ffn_bias
    active = jax.nn.gelu(inner).astype(jnp.bfloat16)
    second_sum = hidden.astype(jnp.float32) + (
        jnp.dot(active, ffn_out, preferred_element_type=jnp.float32) + biases[4]
    )
    output = layer_norm(second_sum, gains[1], biases[5]).astype(jnp.bfloat16)
    picked = cls_index(starts, seq_len)
    kept = (
        flat_tokens,
        joined,
        mixed[picked],
        first_sum[picked],
        hidden[picked],
        inner[picked],
        active[picked],
        second_sum[picked],
    )
    return (output, picked, kept)


def backward(kept, segment, starts, params, upstream):
    attn_in, attn_out, ffn_in, ffn_out, gains, biases, ffn_bias = params
    flat_tokens, joined, mixed_cls, first_cls, hidden_cls, inner_cls, active_cls, second_cls = kept
    batch_size, seq_len = segment.shape
    per_row = starts.shape[1]
    feature = flat_tokens.shape[1]
    head_count = feature // HEAD_DIM
    grad_second, gain_two, shift_two = norm_back(second_cls, gains[1], upstream)
    grad_ffn = grad_second.astype(jnp.bfloat16)
    grad_down = jnp.dot(active_cls.T, grad_ffn, preferred_element_type=jnp.float32)
    grad_active = jnp.dot(grad_ffn, ffn_out.T, preferred_element_type=jnp.float32)
    grad_inner = jax.vjp(jax.nn.gelu, inner_cls)[1](grad_active)[0].astype(jnp.bfloat16)
    grad_up = jnp.dot(hidden_cls.T, grad_inner, preferred_element_type=jnp.float32)
    grad_hidden = grad_second + jnp.dot(grad_inner, ffn_in.T, preferred_element_type=jnp.float32)
    grad_first, gain_one, shift_one = norm_back(first_cls, gains[0], grad_hidden)
    grad_attn = grad_first.astype(jnp.bfloat16)
    grad_outproj = jnp.dot(mixed_cls.T, grad_attn, preferred_element_type=jnp.float32)
    grad_mixed = jnp.dot(grad_attn, attn_out.T, preferred_element_type=jnp.float32).astype(
        jnp.bfloat16
    )
    grad_mixed = grad_mixed.reshape(batch_size, per_row, head_count, HEAD_DIM)
    shaped = joined.reshape(batch_size, seq_len, 3, head_count, HEAD_DIM)
    key_part = shaped[:, :, 1]
    value_part = shaped[:, :, 2]
    picked = cls_index(starts, seq_len)
    query_cls = joined[picked, :feature].reshape(batch_size, per_row, head_count, HEAD_DIM)
    own_seg = jnp.take_along_axis(segment, starts, 1)
    scores = (
        jnp.einsum("bchd,bkhd->bhck", query_cls, key_part, preferred_element_type=jnp.float32)
        * KEY_SCALE
    )
    scores = jnp.where((own_seg[:, :, None] == segment[:, None, :])[:, None], scores, -1000000000.0)
    attention = jax.nn.softmax(scores, -1)
    grad_attention = jnp.einsum(
        "bchd,bkhd->bhck", grad_mixed, value_part, preferred_element_type=jnp.float32
    )
    grad_scores = attention * (
        grad_attention - jnp.sum(attention * grad_attention, -1, keepdims=True)
    )
    grad_scores = grad_scores.astype(jnp.bfloat16)
    grad_query = (
        jnp.einsum("bhck,bkhd->bchd", grad_scores, key_part, preferred_element_type=jnp.float32)
        * KEY_SCALE
    ).astype(jnp.bfloat16)
    grad_key = (
        jnp.einsum("bhck,bchd->bkhd", grad_scores, query_cls, preferred_element_type=jnp.float32)
        * KEY_SCALE
    ).astype(jnp.bfloat16)
    grad_value = jnp.einsum(
        "bhck,bchd->bkhd",
        attention.astype(jnp.bfloat16),
        grad_mixed,
        preferred_element_type=jnp.float32,
    ).astype(jnp.bfloat16)
    places = jnp.arange(seq_len, dtype=jnp.int32)
    selector = (starts[:, :, None] == places[None, None, :]).astype(jnp.bfloat16)
    grad_query_full = jnp.einsum(
        "bcl,bchd->blhd", selector, grad_query, preferred_element_type=jnp.float32
    ).astype(jnp.bfloat16)
    grad_joined = jnp.stack([grad_query_full, grad_key, grad_value], 2).reshape(
        batch_size * seq_len, 3 * feature
    )
    grad_inproj = jnp.dot(flat_tokens.T, grad_joined, preferred_element_type=jnp.float32)
    grad_tokens = (
        jnp.dot(grad_joined, attn_in.T, preferred_element_type=jnp.float32)
        .at[picked]
        .add(grad_first)
    )
    bias_grads = jnp.stack(
        [
            jnp.sum(grad_query.astype(jnp.float32), (0, 1)).reshape(feature),
            jnp.sum(grad_value.astype(jnp.float32), (0, 1)).reshape(feature),
            jnp.sum(grad_attn.astype(jnp.float32), 0),
            shift_one,
            jnp.sum(grad_ffn.astype(jnp.float32), 0),
            shift_two,
        ]
    )
    gain_grads = jnp.stack([gain_one, gain_two])
    hidden_bias = jnp.sum(grad_inner.astype(jnp.float32), 0)
    grads = (grad_inproj, grad_outproj, grad_up, grad_down, gain_grads, bias_grads, hidden_bias)
    row_data = (hidden_cls, grad_inner, active_cls, grad_ffn)
    return (grads, grad_tokens.reshape(batch_size, seq_len, feature), row_data)


def shards(
    query_tokens,
    passage_tokens,
    lengths,
    labels,
    attn_in,
    attn_out,
    ffn_in,
    ffn_out,
    gains,
    biases,
    ffn_bias,
):
    layers = (attn_in, attn_out, ffn_in, ffn_out, gains, biases, ffn_bias)
    query_params = tuple((matrix[0] for matrix in layers))
    passage_params = tuple((matrix[1] for matrix in layers))
    query_count, query_len, feature = query_tokens.shape
    passage_len = passage_tokens.shape[1]
    query_segment = jnp.zeros((query_count, query_len), jnp.int32)
    query_starts = jnp.zeros((query_count, 1), jnp.int32)
    ends = jnp.cumsum(lengths, -1)
    passage_starts = ends - lengths
    places = jnp.arange(passage_len, dtype=jnp.int32)
    passage_segment = jnp.sum((places[None, :, None] >= ends[:, None, :]).astype(jnp.int32), -1)
    query_out, query_pick, query_kept = forward(
        query_tokens, query_segment, query_starts, query_params
    )
    passage_out, passage_pick, passage_kept = forward(
        passage_tokens, passage_segment, passage_starts, passage_params
    )
    query_vec = query_out[query_pick]
    passage_vec = passage_out[passage_pick]
    passage_count = passage_vec.shape[0]
    float_labels = labels.astype(jnp.float32)
    group_vec = lax.all_gather(passage_vec, "grp", axis=0, tiled=True)
    portion = lax.all_gather(group_vec, "blk", axis=0, tiled=True)
    running_max = jnp.full((query_count,), -1e30, jnp.float32)
    score_block = SCORE_SCALE * jnp.dot(query_vec, portion.T, preferred_element_type=jnp.float32)
    column_ids = jnp.arange(portion.shape[0], dtype=jnp.int32)
    new_max = jnp.maximum(running_max, jnp.max(score_block, -1))
    running_sum = jnp.sum(jnp.exp(score_block - new_max[:, None]), -1)
    hits = column_ids[None, :] == labels[:, None]
    positive = jnp.sum(jnp.where(hits, score_block, 0.0), -1)
    running_max, running_sum, positive = (new_max, running_sum, positive)
    norm_log = running_max + jnp.log(running_sum)
    portion = lax.all_gather(group_vec, "blk", axis=0, tiled=True)
    score_block = SCORE_SCALE * jnp.dot(query_vec, portion.T, preferred_element_type=jnp.float32)
    column_ids = jnp.arange(portion.shape[0], dtype=jnp.int32)
    hits = (column_ids[None, :] == labels[:, None]).astype(jnp.float32)
    grad_block = (jnp.exp(score_block - norm_log[:, None]) - hits).astype(jnp.bfloat16)
    query_up = SCORE_SCALE * jnp.dot(grad_block, portion, preferred_element_type=jnp.float32)
    own_ids = (
        lax.axis_index(("blk", "grp")) * passage_count + jnp.arange(passage_count, dtype=jnp.int32)
    ).astype(jnp.float32)
    remote_vec = lax.all_gather(query_vec.astype(jnp.float32), ("blk", "grp"), axis=0, tiled=True)
    remote_log = lax.all_gather(norm_log, ("blk", "grp"), axis=0, tiled=True)
    remote_label = lax.all_gather(float_labels, ("blk", "grp"), axis=0, tiled=True)
    remote_low = remote_vec.astype(jnp.bfloat16)
    score_block = SCORE_SCALE * jnp.dot(
        remote_low, passage_vec.T, preferred_element_type=jnp.float32
    )
    hits = (remote_label[:, None] == own_ids[None, :]).astype(jnp.float32)
    grad_block = (jnp.exp(score_block - remote_log[:, None]) - hits).astype(jnp.bfloat16)
    passage_up = SCORE_SCALE * jnp.dot(grad_block.T, remote_low, preferred_element_type=jnp.float32)
    query_losses = norm_log - positive
    query_grads, query_back, query_rows = backward(
        query_kept, query_segment, query_starts, query_params, query_up
    )
    passage_grads, passage_back, passage_rows = backward(
        passage_kept, passage_segment, passage_starts, passage_params, passage_up
    )
    stacked = tuple(
        (
            jnp.stack([first_part, second_part])
            for first_part, second_part in zip(query_grads, passage_grads)
        )
    )
    grad_win, grad_wout, grad_up, grad_down, grad_gain, grad_bias, grad_hidden_bias = stacked
    shares = (
        lax.psum_scatter(
            grad_win.astype(jnp.bfloat16), "blk", scatter_dimension=1, tiled=True
        ).astype(jnp.float32),
        lax.psum_scatter(
            grad_wout.astype(jnp.bfloat16), "blk", scatter_dimension=1, tiled=True
        ).astype(jnp.float32),
        lax.psum_scatter(
            grad_up.astype(jnp.bfloat16), "blk", scatter_dimension=1, tiled=True
        ).astype(jnp.float32),
        lax.psum_scatter(
            grad_down.astype(jnp.bfloat16), "blk", scatter_dimension=1, tiled=True
        ).astype(jnp.float32),
        lax.psum_scatter(
            grad_gain.astype(jnp.bfloat16), "blk", scatter_dimension=2, tiled=True
        ).astype(jnp.float32),
        lax.psum_scatter(
            grad_bias.astype(jnp.bfloat16), "blk", scatter_dimension=2, tiled=True
        ).astype(jnp.float32),
        lax.psum_scatter(
            grad_hidden_bias.astype(jnp.bfloat16), "blk", scatter_dimension=1, tiled=True
        ).astype(jnp.float32),
    )
    grad_win, grad_wout, grad_up, grad_down, grad_gain, grad_bias, grad_hidden_bias = (
        lax.psum(shares[0].astype(jnp.bfloat16), "grp").astype(jnp.float32),
        lax.psum(shares[1].astype(jnp.bfloat16), "grp").astype(jnp.float32),
        lax.psum(shares[2].astype(jnp.bfloat16), "grp").astype(jnp.float32),
        lax.psum(shares[3].astype(jnp.bfloat16), "grp").astype(jnp.float32),
        lax.psum(shares[4].astype(jnp.bfloat16), "grp").astype(jnp.float32),
        lax.psum(shares[5].astype(jnp.bfloat16), "grp").astype(jnp.float32),
        lax.psum(shares[6].astype(jnp.bfloat16), "grp").astype(jnp.float32),
    )
    query_shaped = query_out.reshape(query_count, query_len, feature)
    passage_shaped = passage_out.reshape(passage_tokens.shape)
    return (
        query_losses,
        query_shaped,
        passage_shaped,
        query_back,
        passage_back,
        grad_win,
        grad_wout,
        grad_up,
        grad_down,
        grad_gain,
        grad_bias,
        grad_hidden_bias,
    )


def solution(mesh):
    placed = (
        P(("blk", "grp"), None, None),
        P(("blk", "grp"), None, None),
        P(("blk", "grp"), None),
        P(("blk", "grp")),
        P(),
        P(),
        P(),
        P(),
        P(),
        P(),
        P(),
    )
    return jax.shard_map(
        shards,
        mesh=mesh,
        in_specs=placed,
        out_specs=(
            P(("blk", "grp")),
            P(("blk", "grp"), None, None),
            P(("blk", "grp"), None, None),
            P(("blk", "grp"), None, None),
            P(("blk", "grp"), None, None),
            P(None, "blk", None),
            P(None, "blk", None),
            P(None, "blk", None),
            P(None, "blk", None),
            P(None, None, "blk"),
            P(None, None, "blk"),
            P(None, "blk"),
        ),
        check_vma=False,
    )
```

profile of v0, /device:TPU:9, one launch (start us, length us, event | category | flops | bytes accessed | tf_op | source)
XLA Modules:
  0.0 1674.8 jit_solution(13967062988657082071)
XLA Ops:
  11.1 8.4 add_convert_fusion.1
  19.5 15.1 reshape.413
  34.5 5.9 fusion.198
  42.4 14.1 fusion.201
  61.7 6.1 convert_element_type.251
  72.7 12.7 fusion.14
  85.5 5.3 fusion.203
  98.0 87.7 %while.2 = (s32[]{:T(128)}, bf16[1024,2304]{1,0:T(8,128)(2,1)}, s32[32,2]{0,1:T(2,128)S(1)}, bf16[32,768]{1,0:T(8,128)(2,1)S(1)}, s32[]{:T(128)}, /*index=5*/s32[]{:T(128)}) while((s32[]{:T(128)}, bf16[1024,2304]{1,0:T(8,128)(2,1)}, s32[32,2]{0,1:T(2,128)S(1)}, bf16[32,768]{1,0:T(8,128)(2,1)S(1)}, s32[]{:T(128)}, /*index=5*/s32[]{:T(128)}) %tuple.105), condition=%wide.while_cond, body=%wide.while_body.sunk | while | flops 2 | bytes 6265 | solution.py:110
  193.0 8.5 add_convert_fusion
  201.5 6.6 copy.80
  208.1 8.8 reshape.415
  217.0 5.9 fusion.199
  224.1 6.2 gather_fusion.4
  231.1 14.7 fusion.204
  245.8 10.0 fusion.85
  261.4 12.4 fusion.22
  273.9 9.9 fusion.206
  291.9 29.9 %all-gather.1 = bf16[256,768]{1,0:T(8,128)(2,1)S(1)} all-gather(bf16[16,768]{1,0:T(8,128)(2,1)S(1)} %all-gather), channel_id=3, replica_groups=mesh['blk'=16,'grp'=2] {'blk'}, dimensions={0}, use_global_device_ids=true | all-gather | bytes 417792 | tf_op jit(solution)/shard_map/all_gather | solution.py:205
  327.4 4.6 fusion.212
  332.1 4.6 multiply_reduce_fusion.7
  338.3 22.1 %while.3 = (s32[]{:T(128)}, bf16[1024,2304]{1,0:T(8,128)(2,1)}, s32[8,2]{0,1:T(2,128)S(1)}, bf16[8,768]{1,0:T(8,128)(2,1)S(1)}, s32[]{:T(128)}, /*index=5*/s32[]{:T(128)}) while((s32[]{:T(128)}, bf16[1024,2304]{1,0:T(8,128)(2,1)}, s32[8,2]{0,1:T(2,128)S(1)}, bf16[8,768]{1,0:T(8,128)(2,1)S(1)}, s32[]{:T(128)}, /*index=5*/s32[]{:T(128)}) %tuple.130), condition=%wide.while_cond.1, body=%wide.while_body.1.sunk | while | flops 2 | bytes 6265 | solution.py:110
  365.0 6.1 gather_fusion.7
  386.1 6.4 pad_maximum_fusion
  392.5 15.7 reshape.422
  408.4 51.0 %all-reduce.5 = (f32[1024]{0:T(1024)}, f32[1024]{0:T(1024)}) all-reduce(f32[1024]{0:T(1024)S(1)} %convert_dynamic-update-slice_fusion, f32[1024]{0:T(1024)S(1)} %get-tuple-element.145), channel_id=1, replica_groups=mesh['blk'=16,'grp'=2] {'blk','grp'}, use_global_device_ids=true, to_apply=%add.3 | all-reduce | flops 2048 | bytes 16384
  464.6 6.7 fusion.46
  471.3 4.2 multiply_reduce_fusion.15
  477.7 4.3 fusion.211
  482.0 4.4 multiply_reduce_fusion.16
  504.8 9.4 copy.90
  520.4 4.1 fusion.47
  528.0 18.2 %copy.91 = bf16[2,768,2304]{2,0,1:T(2,128)(2,1)} copy(bf16[2,768,2304]{1,2,0:T(8,128)(2,1)} %pad_maximum_fusion.3) | data formatting | bytes 14155776 | tf_op jit(solution)/shard_map/stack | solution.py:243
  553.3 4.6 gather_fusion.12
  557.9 4.4 gather_fusion.13
  569.6 8.4 pad_maximum_fusion.2
  590.4 8.3 pad_maximum_fusion.1
  608.9 163.1 %all-reduce.11.cloned.1.call-done = bf16[2,768,2304]{2,0,1:T(2,128)(2,1)} async-done(((bf16[2,768,2304]{2,0,1:T(2,128)(2,1)}), bf16[2,768,2304]{2,0,1:T(2,128)(2,1)}) %all-reduce.11.cloned.1.call-update) | async-done | bytes 7077904
  774.1 129.3 %reduce-scatter.13.cloned.1.call-done = bf16[2,48,768]{2,1,0:T(8,128)(2,1)} async-done(((bf16[2,768,768]{2,1,0:T(8,128)(2,1)}), bf16[2,48,768]{2,1,0:T(8,128)(2,1)}) %reduce-scatter.13.cloned.1.call-update) | async-done | bytes 147472 | tf_op jit(solution)/shard_map/reduce_scatter | solution.py:252
  903.4 176.2 %reduce-scatter.17.cloned.1.call-done = bf16[2,192,768]{2,1,0:T(8,128)(2,1)} async-done(((bf16[2,3072,768]{2,1,0:T(8,128)(2,1)}), bf16[2,192,768]{2,1,0:T(8,128)(2,1)}) %reduce-scatter.17.cloned.1.call-update) | async-done | bytes 589840 | tf_op jit(solution)/shard_map/reduce_scatter | solution.py:258
  1079.7 175.8 %reduce-scatter.15.cloned.1.call-done = bf16[2,48,3072]{2,1,0:T(8,128)(2,1)} async-done(((bf16[2,768,3072]{2,1,0:T(8,128)(2,1)}), bf16[2,48,3072]{2,1,0:T(8,128)(2,1)}) %reduce-scatter.15.cloned.1.call-update) | async-done | bytes 589840 | tf_op jit(solution)/shard_map/reduce_scatter | solution.py:255
  1255.5 6.8 fusion.66
  1264.2 10.1 fusion.63
  1274.3 4.2 scatter_fusion.1
  1278.5 102.5 %reduce-scatter.19.cloned.1.call-done = bf16[48,4]{1,0:T(8,128)(2,1)} async-done(((bf16[768,4]{1,0:T(8,128)(2,1)}), bf16[48,4]{1,0:T(8,128)(2,1)}) %reduce-scatter.19.cloned.1.call-update) | async-done | bytes 400
  1381.9 126.8 %reduce-scatter.23.cloned.1.call-done = bf16[192,2]{1,0:T(8,128)(2,1)} async-done(((bf16[3072,2]{1,0:T(8,128)(2,1)}), bf16[192,2]{1,0:T(8,128)(2,1)}) %reduce-scatter.23.cloned.1.call-update) | async-done | bytes 784
  1509.6 125.2 %reduce-scatter.21.cloned.1.call-done = bf16[48,12]{1,0:T(8,128)(2,1)} async-done(((bf16[768,12]{1,0:T(8,128)(2,1)}), bf16[48,12]{1,0:T(8,128)(2,1)}) %reduce-scatter.21.cloned.1.call-update) | async-done | bytes 1168
  1635.7 4.8 all-reduce.6
  1642.3 18.7 %all-reduce.13.cloned.1.call-done = (bf16[2,48,2304]{2,0,1:T(2,128)(2,1)}, bf16[2,48,768]{2,1,0:T(8,128)(2,1)}, bf16[2,48,3072]{2,1,0:T(8,128)(2,1)}, bf16[2,192,768]{2,1,0:T(8,128)(2,1)}) async-done(((bf16[2,48,2304]{2,0,1:T(2,128)(2,1)}, bf16[2,48,768]{2,1,0:T(8,128)(2,1)}, bf16[2,48,3072]{2,1,0:T(8,128)(2,1)}, bf16[2,192,768]{2,1,0:T(8,128)(2,1)}), (bf16[2,48,2304]{2,0,1:T(2,128)(2,1)}, ...) | async-done | bytes 1769488 | tf_op jit(solution)/shard_map/psum | solution.py:272
  (555 shorter events, 267.6 us)
Async XLA Ops:
  7.2 464.2 %all-gather.4.cloned.1.call-start = ((), (), s32[]{:S(2)}) async-start(), calls=%async_computation.6 | async-start | bytes 1622016 | tf_op jit(solution)/shard_map/all_gather | solution.py:224
  7.3 216.8 %copy-start.48 = (s32[1024]{0:T(1024)}, s32[1024]{0:T(1024)S(1)}, u32[]{:S(2)}) copy-start(s32[1024]{0:T(1024)S(1)} %pad_clamp_fusion.1) | copy-start | bytes 12292
  40.5 16.1 copy-start.5
  72.1 13.4 slice-start
  72.7 12.8 copy-start.6
  72.7 12.8 slice-start.1
  72.7 12.8 slice-start.2
  90.8 6.8 copy-start.70
  97.1 674.9 %all-reduce.11.cloned.1.call-start = ((), (), s32[]{:S(2)}) async-start(), calls=%async_computation.13 | async-start | bytes 14155776
  97.8 103.7 %copy-start.50 = (s32[2,4]{1,0:T(2,128)}, s32[2,4]{1,0:T(2,128)S(1)}, u32[]{:S(2)}) copy-start(s32[2,4]{1,0:T(2,128)S(1)} %get-tuple-element.144) | copy-start | bytes 100
  193.0 8.5 copy-start.79
  193.0 67.3 %copy-start.47 = (s32[1024]{0:T(1024)}, s32[1024]{0:T(1024)S(1)}, u32[]{:S(2)}) copy-start(s32[1024]{0:T(1024)S(1)} %pad_clamp_fusion) | copy-start | bytes 12292
  222.8 23.0 %copy-start.15 = (bf16[2,512,1,12,64]{1,0,4,3,2:T(2,128)(2,1)}, bf16[2,512,1,12,64]{1,0,4,3,2:T(2,128)(2,1)S(1)}, u32[]{:S(2)}) copy-start(bf16[2,512,1,12,64]{1,0,4,3,2:T(2,128)(2,1)S(1)} %get-tuple-element.156) | copy-start | bytes 4718596
  222.8 23.0 %copy-start.17 = (bf16[2,512,1,12,64]{1,0,4,3,2:T(2,128)(2,1)}, bf16[2,512,1,12,64]{1,0,4,3,2:T(2,128)(2,1)S(1)}, u32[]{:S(2)}) copy-start(bf16[2,512,1,12,64]{1,0,4,3,2:T(2,128)(2,1)S(1)} %get-tuple-element.154) | copy-start | bytes 4718596
  223.0 22.9 %copy-start.74 = (f32[32]{0:T(128)}, f32[32]{0:T(128)S(1)}, u32[]{:S(2)}) copy-start(f32[32]{0:T(128)S(1)} %broadcast_multiply_fusion.17) | copy-start | bytes 388
  230.4 15.5 copy-start.63
  260.9 199.2 %copy-start.22 = (f32[8,768]{1,0:T(8,128)}, f32[8,768]{1,0:T(8,128)S(1)}, u32[]{:S(2)}) copy-start(f32[8,768]{1,0:T(8,128)S(1)} %gather_fusion.5) | copy-start | bytes 73732
  261.4 12.4 copy-start.14
  261.4 12.4 copy-start.71
  273.8 9.9 copy-start.45
  273.9 11.2 copy-start.41
  284.5 175.8 %copy-start.24 = (f32[8,768]{1,0:T(8,128)}, f32[8,768]{1,0:T(8,128)S(1)}, u32[]{:S(2)}) copy-start(f32[8,768]{1,0:T(8,128)S(1)} %gather_fusion.6) | copy-start | bytes 73732
  327.4 9.3 copy-start.29
  332.1 28.5 %copy-start.40 = (bf16[32,12,64,1]{2,3,1,0:T(2,128)(2,1)S(1)}, bf16[32,12,64,1]{2,3,1,0:T(2,128)(2,1)}, u32[]{:S(2)}) copy-start(bf16[32,12,64,1]{2,3,1,0:T(2,128)(2,1)} %reshape.620) | copy-start | bytes 147460
  337.3 27.6 %copy-start.18 = (f32[32,768]{1,0:T(8,128)}, f32[32,768]{1,0:T(8,128)S(1)}, u32[]{:S(2)}) copy-start(f32[32,768]{1,0:T(8,128)S(1)} %get-tuple-element.138) | copy-start | bytes 294916
  360.5 101.6 %copy-start.43 = (bf16[2,4,12,64]{3,2,1,0:T(8,128)(2,1)}, bf16[2,4,12,64]{3,2,1,0:T(8,128)(2,1)S(1)}, u32[]{:S(2)}) copy-start(bf16[2,4,12,64]{3,2,1,0:T(8,128)(2,1)S(1)} %reshape.425) | copy-start | bytes 36868
  365.0 17.5 %copy-start.12 = (f32[32,12,32]{1,2,0:T(8,128)}, f32[32,12,32]{1,2,0:T(8,128)S(1)}, u32[]{:S(2)}) copy-start(f32[32,12,32]{1,2,0:T(8,128)S(1)} %get-tuple-element.183) | copy-start | bytes 147460
  371.2 11.3 copy-start.7
  392.4 69.0 %copy-start.42 = (f32[768]{0:T(1024)S(1)}, f32[768]{0:T(1024)}, u32[]{:S(2)}) copy-start(f32[768]{0:T(1024)} %get-tuple-element.106) | copy-start | bytes 9220
  392.4 69.6 %copy-start.69 = (s32[2,4]{1,0:T(2,128)S(1)}, s32[2,4]{1,0:T(2,128)}, u32[]{:S(2)}) copy-start(s32[2,4]{1,0:T(2,128)} %get-tuple-element.161) | copy-start | bytes 100
  392.4 69.7 %copy-start.16 = (bf16[2,512,1,12,64]{1,0,4,3,2:T(2,128)(2,1)S(1)}, bf16[2,512,1,12,64]{1,0,4,3,2:T(2,128)(2,1)}, u32[]{:S(2)}) copy-start(bf16[2,512,1,12,64]{1,0,4,3,2:T(2,128)(2,1)} %copy-done.15) | copy-start | bytes 4718596
  477.7 8.8 copy-start.31
  546.3 357.1 %reduce-scatter.13.cloned.1.call-start = ((), (), s32[]{:S(2)}) async-start(), calls=%async_computation.7 | async-start | bytes 2506752 | tf_op jit(solution)/shard_map/reduce_scatter | solution.py:252
  551.3 11.0 copy-start.30
  553.1 12.9 copy-start.32
  553.1 526.6 %reduce-scatter.17.cloned.1.call-start = ((), (), s32[]{:S(2)}) async-start(), calls=%async_computation.9 | async-start | bytes 10027008 | tf_op jit(solution)/shard_map/reduce_scatter | solution.py:258
  578.0 8.8 copy-start.34
  578.1 677.4 %reduce-scatter.15.cloned.1.call-start = ((), (), s32[]{:S(2)}) async-start(), calls=%async_computation.8 | async-start | bytes 10027008 | tf_op jit(solution)/shard_map/reduce_scatter | solution.py:255
  598.9 6.8 copy-start.56
  598.9 6.8 copy-start.67
  598.9 8.1 copy-start.68
  598.9 782.1 %reduce-scatter.19.cloned.1.call-start = ((), (), s32[]{:S(2)}) async-start(), calls=%async_computation.10 | async-start | bytes 208896
  605.5 903.2 %reduce-scatter.23.cloned.1.call-start = ((), (), s32[]{:S(2)}) async-start(), calls=%async_computation.12 | async-start | bytes 835584
  607.1 1027.7 %reduce-scatter.21.cloned.1.call-start = ((), (), s32[]{:S(2)}) async-start(), calls=%async_computation.11 | async-start | bytes 208896
  608.6 1052.4 %all-reduce.13.cloned.1.call-start = ((), (), s32[]{:S(2)}) async-start(), calls=%async_computation.14 | async-start | bytes 3538944 | tf_op jit(solution)/shard_map/psum | solution.py:272
  1255.4 6.8 copy-start.78
  1264.2 10.1 copy-start.37
  1264.2 10.1 copy-start.80
  (56 other events, 207.6 us)
Sparse Core Ops, SparseCore 0:
  97.2 55.6 all-gather.3
  546.4 225.5 all-reduce.10
  777.5 125.8 reduce-scatter.12
  909.9 169.7 reduce-scatter.16
  1085.2 170.1 reduce-scatter.14
  1261.2 119.7 reduce-scatter.18
  1387.0 121.7 reduce-scatter.22
  1514.6 120.1 reduce-scatter.20
  1638.2 22.8 all-reduce.12
where the time goes:
time: 1680 us; the launch traced here: 1670 us
  waiting for transfers between devices  1020 us (61%)
  local copies, waits for them, and re-layouts  275 us (16%)
  matrix products  183 us (11%)
  other arithmetic  92.2 us (5%)
  blocking collectives  88 us (5%)
    unnamed x13, waiting for transfers between devices  518 us
    reduce_scatter x1, waiting for transfers between devices, shards(): lax.psum_scatter(grad_down.astype(jnp.bfloat16), 'blk', scatter_dimension...  176 us
    reduce_scatter x1, waiting for transfers between devices, shards(): lax.psum_scatter(grad_up.astype(jnp.bfloat16), 'blk', scatter_dimension=1...  176 us
    reduce_scatter x1, waiting for transfers between devices, shards(): lax.psum_scatter(grad_wout.astype(jnp.bfloat16), 'blk', scatter_dimension...  129 us
    gather x160, local copies, waits for them, and re-layouts  109 us
    unnamed x1, blocking collectives  51 us
  transfers between devices with their start and end apart: 9, of which 8 were waited for; matrix products, arithmetic and copies ran while one was open for 23% of the time, Pallas kernels for 0%

commit v1 on v0

--- a/solution.py
+++ b/solution.py
@@ -1,14 +1,910 @@
+import functools
 import jax
 import jax.numpy as jnp
 from jax import lax
+from jax.experimental import pallas as pl
+from jax.experimental.pallas import tpu as pltpu
 from jax.sharding import PartitionSpec as P
 
+MESH = pl.DeviceIdType.MESH
 HEAD_DIM = 64
-
-
+HEADS = 12
 EPSILON = 1e-05
 SCORE_SCALE = 0.08
 KEY_SCALE = 0.125
+NEG = -1000000000.0
+F32 = jnp.float32
+BF16 = jnp.bfloat16
+VMEM_LIMIT = 60 * 1024 * 1024
+
+
+def dot(a, b):
+    return lax.dot_general(a, b, (((1,), (0,)), ((), ())), preferred_element_type=F32)
+
+
+def dot_nt(a, b):
+    return lax.dot_general(a, b, (((1,), (1,)), ((), ())), preferred_element_type=F32)
+
+
+def dot_tn(a, b):
+    return lax.dot_general(a, b, (((0,), (0,)), ((), ())), preferred_element_type=F32)
+
+
+def iota(shape, dim):
+    return lax.broadcasted_iota(jnp.int32, shape, dim)
+
+
+def head_row(h):
+    return iota((1, 768), 1) // HEAD_DIM == h
+
+
+def expand_heads(rows):
+    return jnp.concatenate(
+        [jnp.where(head_row(h), rows, 0.0) for h in range(HEADS)], 0
+    )
+
+
+def fold_heads(rows, count):
+    out = jnp.where(head_row(0), rows[:count], 0.0)
+    for h in range(1, HEADS):
+        out = out + jnp.where(head_row(h), rows[h * count:(h + 1) * count], 0.0)
+    return out
+
+
+def norm_stats(residual):
+    centre = residual - jnp.mean(residual, -1, keepdims=True)
+    inverse = lax.rsqrt(jnp.mean(centre * centre, -1, keepdims=True) + EPSILON)
+    return centre * inverse, inverse
+
+
+def gelu(v):
+    return 0.5 * v * (1.0 + jnp.tanh(0.7978845608028654 * (v + 0.044715 * (v * v * v))))
+
+
+def split3(v):
+    hi = v.astype(BF16).astype(F32)
+    rest = v - hi
+    mid = rest.astype(BF16).astype(F32)
+    return hi, mid, rest - mid
+
+
+def lane_pack(columns, count):
+    lane = iota((count, 128), 1)
+    out = jnp.zeros((count, 128), F32)
+    for j, column in enumerate(columns):
+        out = jnp.where(lane == j, column, out)
+    return out
+
+
+def norm_back(up, gain, normed, inverse):
+    u = up * gain
+    return inverse * (
+        u - jnp.mean(u, -1, keepdims=True) - normed * jnp.mean(u * normed, -1, keepdims=True)
+    )
+
+
+def gelu_pair(v):
+    sq = v * v
+    th = jnp.tanh(0.7978845608028654 * (v + 0.044715 * (v * sq)))
+    half = 0.5 * (1.0 + th)
+    slope = half + 0.5 * v * (1.0 - th * th) * (0.7978845608028654 * (1.0 + 0.134145 * sq))
+    return v * half, slope
+
+
+def decode_inv(ext):
+    return ext[:, 0:1] + ext[:, 1:2] + ext[:, 2:3], ext[:, 3:4] + ext[:, 4:5] + ext[:, 5:6]
+
+
+def ext_rows(block):
+    e_p = block[:, :, 0:128].reshape(128, 128)
+    e_q = jnp.concatenate([block[:, :, 128 * a:128 * a + 128] for a in range(1, 5)], 1)
+    return e_p, e_q.reshape(512, 128)
+
+
+def place():
+    return lax.axis_index("blk"), lax.axis_index("grp")
+
+
+def remote(src, dst, send, recv, peer):
+    return pltpu.make_async_remote_copy(
+        src_ref=src, dst_ref=dst, send_sem=send, recv_sem=recv, device_id=peer, device_id_type=MESH
+    )
+
+
+def greet(me, g):
+    barrier = pltpu.get_barrier_semaphore()
+    for i in range(1, 16):
+        pl.semaphore_signal(barrier, inc=1, device_id=(lax.rem(me + i, 16), g), device_id_type=MESH)
+    pl.semaphore_signal(barrier, inc=1, device_id=(me, 1 - g), device_id_type=MESH)
+
+
+def greeted():
+    pl.semaphore_wait(pltpu.get_barrier_semaphore(), 16)
+
+
+def gather_phases(me, g, pay, ga, ss, rs, base, lo, hi):
+    z, yx = me // 4, lax.rem(me, 4)
+    xpeer = me + 1 - 2 * lax.rem(me, 2)
+    ypeer = me + 2 - 4 * (lax.rem(me, 4) // 2)
+    yx_x, yx_y = lax.rem(xpeer, 4), lax.rem(ypeer, 4)
+    rows = slice(lo, hi)
+    first, second, third = [], [], []
+
+    def add(phase, src, dst, k, peer):
+        phase.append(remote(src, dst, ss.at[base + k], rs.at[base + k], (peer, g)))
+
+    for d in range(1, 4):
+        peer = lax.rem(z + d, 4) * 4 + yx
+        add(first, pay.at[rows], ga.at[z, yx, rows], d - 1, peer)
+    add(second, ga.at[:, yx, rows], ga.at[:, yx, rows], 3, xpeer)
+    add(second, ga.at[:, yx, rows], ga.at[:, yx, rows], 4, ypeer)
+    add(third, ga.at[0:2, yx_x, rows], ga.at[0:2, yx_x, rows], 5, ypeer)
+    add(third, ga.at[2:4, yx_y, rows], ga.at[2:4, yx_y, rows], 6, xpeer)
+    return first, second, third
+
+
+def forward_kernel(
+    lens_ref, labels_ref, gains_ref, biases_ref, ffnb_ref,
+    xq_hbm, xp_hbm, win_hbm, wout_hbm, fin_hbm, fout_hbm,
+    out_hbm, ga_hbm, rsw_ref, part_hbm, uw_hbm, dspq_hbm, dspp_hbm,
+    loss_ref, upq_ref, upp_ref, gq_ref, yt_ref, ext_ref,
+    x_s, q_s, kv_s, win_s, wout_s, fin_s, fout_s, pq_s, pp_s, out_s, mix_s, bias_s,
+    pay_s, swap_s, ga_ref, gs_ref, innq_ref, innp_ref, invq_ref, invp_ref, qq_ref, zq_ref, loss_s,
+    sem, lsem, osem, ss, rs, as_, ar,
+):
+    me, g = place()
+    z, yx = me // 4, lax.rem(me, 4)
+    greet(me, g)
+    copies = []
+    for t, x_hbm in enumerate((xq_hbm, xp_hbm)):
+        copies.append([
+            pltpu.make_async_copy(x_hbm, x_s.at[t], sem.at[t, 0]),
+            pltpu.make_async_copy(win_hbm.at[t], win_s.at[t], sem.at[t, 1]),
+            pltpu.make_async_copy(wout_hbm.at[t], wout_s.at[t], sem.at[t, 2]),
+            pltpu.make_async_copy(fin_hbm.at[t], fin_s.at[t], sem.at[t, 3]),
+            pltpu.make_async_copy(fout_hbm.at[t], fout_s.at[t], sem.at[t, 4]),
+        ])
+    for c in copies[0][:2] + copies[1][:2] + copies[0][2:] + copies[1][2:]:
+        c.start()
+    a1, b1, c1 = gather_phases(me, g, pay_s, ga_ref, ss, rs, 0, 0, 64)
+    a2, b2, c2 = gather_phases(me, g, pay_s, ga_ref, ss, rs, 7, 64, 96)
+    last_hop = [remote(ga_ref.at[:, :, 0:64], gs_ref, ss.at[14], rs.at[14], (me, 1 - g))]
+    swaps = []
+    for i in range(1, 16):
+        peer = lax.rem(me + i, 16)
+        swaps.append(remote(swap_s.at[peer], rsw_ref.at[me], as_.at[i], ar.at[i], (peer, g)))
+    own_copy = [
+        pltpu.make_async_copy(pay_s, ga_ref.at[z, yx], lsem.at[0]),
+        pltpu.make_async_copy(swap_s.at[me], rsw_ref.at[me], lsem.at[1]),
+    ]
+
+    tokens = x_s.shape[1]
+    col_q = iota((32, tokens), 1)
+    row_q = iota((32, tokens), 0)
+    sel_q = col_q == row_q * 32
+    own_q = col_q // 32 == row_q
+    col_p = iota((8, tokens), 1)
+    row_p = iota((8, tokens), 0)
+    lo = jnp.zeros((8, tokens), jnp.int32)
+    hi = jnp.zeros((8, tokens), jnp.int32)
+    for r in range(2):
+        acc = jnp.int32(r * 512)
+        for c in range(4):
+            length = lens_ref[r, c]
+            lo = jnp.where(row_p == r * 4 + c, acc, lo)
+            acc = acc + length
+            hi = jnp.where(row_p == r * 4 + c, acc, hi)
+    sel_p = col_p == lo
+    own_p = (col_p >= lo) & (col_p < hi)
+
+    picks = []
+    for t, sel in enumerate((sel_q, sel_p)):
+        copies[t][0].wait()
+        copies[t][1].wait()
+        query_bias = biases_ref[0, t:t + 1, :]
+        value_bias = biases_ref[1, t:t + 1, :]
+
+        def kv_step(m, _, t=t, query_bias=query_bias, value_bias=value_bias):
+            rows = pl.ds(pl.multiple_of(m * 256, 256), 256)
+            x = x_s[t, rows, :]
+            kv_s[t, rows, 0:768] = dot(x, win_s[t, :, 768:1536]).astype(BF16)
+            kv_s[t, rows, 768:1536] = (dot(x, win_s[t, :, 1536:2304]) + value_bias).astype(BF16)
+            q_s[t, rows, :] = (dot(x, win_s[t, :, 0:768]) + query_bias).astype(BF16)
+            return 0
+
+        lax.fori_loop(0, tokens // 256, kv_step, 0)
+        pick = jnp.where(sel, 1.0, 0.0).astype(BF16)
+        picks.append((dot(pick, x_s[t]), dot(pick, q_s[t])))
+
+    done = []
+    for t, (own, count, p_s, inn_ref, inv_ref) in enumerate((
+        (own_q, 32, pq_s, innq_ref, invq_ref), (own_p, 8, pp_s, innp_ref, invp_ref),
+    )):
+        xc, qc = picks[t]
+        scores = dot_nt(expand_heads(qc).astype(BF16), kv_s[t, :, 0:768]) * KEY_SCALE
+        own12 = jnp.concatenate([jnp.where(own, 0.0, NEG)] * HEADS, 0)
+        scores = scores + own12
+        weight = jnp.exp(scores - jnp.max(scores, -1, keepdims=True))
+        soft = weight * (1.0 / jnp.sum(weight, -1, keepdims=True))
+        p_s[...] = soft
+        soft16 = soft.astype(BF16)
+        mixed = fold_heads(dot(soft16, kv_s[t, :, 768:1536]), count).astype(BF16)
+        zsum = dot(soft16, x_s[t])
+        copies[t][2].wait()
+        first = xc + (dot(mixed, wout_s[t]) + biases_ref[2, t:t + 1, :])
+        n1, inv1 = norm_stats(first)
+        hidden = (n1 * gains_ref[t, 0:1, :] + biases_ref[3, t:t + 1, :]).astype(BF16)
+        copies[t][3].wait()
+        inner = dot(hidden, fin_s[t]) + ffnb_ref[t:t + 1, :]
+        inn_ref[...] = inner
+        active = gelu(inner).astype(BF16)
+        copies[t][4].wait()
+        second = hidden.astype(F32) + (dot(active, fout_s[t]) + biases_ref[4, t:t + 1, :])
+        n2, inv2 = norm_stats(second)
+        vec = (n2 * gains_ref[t, 1:2, :] + biases_ref[5, t:t + 1, :]).astype(BF16)
+        inv_ref[...] = lane_pack([inv1, inv2], count)
+        if t == 0:
+            zq_ref[...] = zsum.astype(BF16)
+        else:
+            wide = jnp.concatenate([zsum, jnp.zeros((32, 768), F32)], 0)
+            swap_s[:, 48:96, :] = wide.T.astype(BF16).reshape(16, 48, 128)
+        done.append((xc, qc, mixed, hidden, vec, inv1, inv2))
+
+    xq, qq, mq, hq, vq, i1q, i2q = done[0]
+    xp, qp, mp, hp, vp, i1p, i2p = done[1]
+    lab = labels_ref[...].astype(F32)
+    eye = iota((32, 32), 0) == iota((32, 32), 1)
+    lab_col = jnp.sum(jnp.where(eye, lab, 0.0), 1, keepdims=True)
+    lab_hi = jnp.floor(lab_col * (1.0 / 256.0))
+    lab_lo = lab_col - 256.0 * lab_hi
+    ext_q = lane_pack([*split3(i1q), *split3(i2q), lab_hi, lab_lo], 32)
+    ext_p = lane_pack([*split3(i1p), *split3(i2p)], 8)
+    ext = jnp.concatenate(
+        [ext_p] + [ext_q[8 * a:8 * a + 8] for a in range(4)] + [jnp.zeros((8, 128), F32)], 1
+    )
+    pay_s[0:32, :] = vq
+    pay_s[32:64, :] = jnp.concatenate([hp.astype(F32), vp.astype(F32), qp, ext], 0).astype(BF16)
+    pay_s[64:96, :] = hq
+    qq_ref[...] = qq.astype(BF16)
+    greeted()
+    own_copy[0].start()
+    for c in a1 + a2:
+        c.start()
+    m48 = jnp.concatenate([mq.astype(F32), mp.astype(F32), jnp.zeros((8, 768), F32)], 0)
+    x48 = jnp.concatenate([xq, xp, jnp.zeros((8, 768), F32)], 0)
+    swap_s[:, 0:48, :] = jnp.zeros((16, 48, 128), BF16)
+    for b in range(16):
+        swap_s[b, 0:48, 0:48] = m48[:, 48 * b:48 * b + 48].astype(BF16)
+        swap_s[b, 0:48, 64:112] = x48[:, 48 * b:48 * b + 48].astype(BF16)
+    for c in own_copy[1:]:
+        c.start()
+
+    low_half = iota((1, 128), 1) < HEAD_DIM
+
+    def tile(step, _):
+        tower = step // 4
+        rows = pl.ds(pl.multiple_of(lax.rem(step, 4) * 256, 256), 256)
+
+        def on(k, waits, starts):
+            @pl.when(step == k)
+            def _():
+                for c in waits:
+                    c.wait()
+                for c in starts:
+                    c.start()
+
+        on(1, own_copy[0:1] + a1, b1)
+        on(2, a2, b2 + swaps)
+        on(3, b1, c1)
+        on(4, b2, c2)
+        on(5, c1, last_hop)
+
+        @pl.when(step < 4)
+        def _():
+            same = iota((128, 128), 0) // 32 == iota((128, 128), 1) // 32
+            mask = jnp.where(same, 0.0, NEG)
+            mask2 = jnp.concatenate([mask, mask], 0)
+            for part in range(2):
+                at = pl.ds(pl.multiple_of(lax.rem(step, 4) * 256 + part * 128, 128), 128)
+                for j in range(HEADS // 2):
+                    lanes = slice(128 * j, 128 * j + 128)
+                    q = q_s[0, at, lanes]
+                    k = kv_s[0, at, lanes]
+                    v = kv_s[0, at, 768 + 128 * j:768 + 128 * j + 128]
+                    zero = jnp.zeros_like(q)
+                    q2 = jnp.concatenate([jnp.where(low_half, q, zero), jnp.where(low_half, zero, q)], 0)
+                    s = dot_nt(q2, k) * KEY_SCALE + mask2
+                    e = jnp.exp(s - jnp.max(s, -1, keepdims=True))
+                    total = jnp.sum(e, -1, keepdims=True)
+                    o = dot(e.astype(BF16), v) * (1.0 / total)
+                    mix_s[part * 128:part * 128 + 128, lanes] = jnp.where(low_half, o[:128], o[128:]).astype(BF16)
+
+        @pl.when(step >= 4)
+        def _():
+            row = (step - 4) // 2
+            base = lax.rem(step, 2) * 256
+            keys = pl.ds(pl.multiple_of(row * 512, 512), 512)
+            qpos = iota((256, 512), 0) + base
+            kpos = iota((256, 512), 1)
+            qseg = jnp.zeros((256, 512), jnp.int32)
+            kseg = jnp.zeros((256, 512), jnp.int32)
+            end = jnp.int32(0)
+            for c in range(3):
+                end = end + lens_ref[row, c]
+                qseg = qseg + jnp.where(qpos >= end, 1, 0)
+                kseg = kseg + jnp.where(kpos >= end, 1, 0)
+            mask = jnp.where(qseg == kseg, 0.0, NEG)
+            bias_s[...] = mask
+            for j in range(HEADS // 2):
+                lanes = slice(128 * j, 128 * j + 128)
+                q = q_s[1, rows, lanes]
+                k = kv_s[1, keys, lanes]
+                v = kv_s[1, keys, 768 + 128 * j:768 + 128 * j + 128]
+                zero = jnp.zeros_like(q)
+                q2 = jnp.concatenate([jnp.where(low_half, q, zero), jnp.where(low_half, zero, q)], 0)
+                s = dot_nt(q2, k) * KEY_SCALE
+                s = jnp.concatenate([s[:256] + bias_s[...], s[256:] + bias_s[...]], 0)
+                e = jnp.exp(s - jnp.max(s, -1, keepdims=True))
+                total = jnp.sum(e, -1, keepdims=True)
+                o = dot(e.astype(BF16), v) * (1.0 / total)
+                mix_s[:, lanes] = jnp.where(low_half, o[:256], o[256:]).astype(BF16)
+
+        first_sum = x_s[tower, rows, :].astype(F32) + (
+            dot(mix_s[...], wout_s[tower]) + biases_ref[2, pl.ds(tower, 1), :]
+        )
+        n1, _ = norm_stats(first_sum)
+        hidden = (n1 * gains_ref[tower, 0:1, :] + biases_ref[3, pl.ds(tower, 1), :]).astype(BF16)
+        second_sum = hidden.astype(F32) + biases_ref[4, pl.ds(tower, 1), :]
+        for c in range(4):
+            cols = slice(768 * c, 768 * c + 768)
+            inner = dot(hidden, fin_s[tower, :, cols]) + ffnb_ref[pl.ds(tower, 1), cols]
+            second_sum = second_sum + dot(gelu(inner).astype(BF16), fout_s[tower, cols, :])
+        n2, _ = norm_stats(second_sum)
+        slot = lax.rem(step, 2)
+
+        @pl.when(step >= 2)
+        def _():
+            pltpu.make_async_copy(out_s.at[slot], out_hbm.at[tower, rows], osem.at[slot]).wait()
+
+        out_s[slot] = (
+            n2 * gains_ref[tower, 1:2, :] + biases_ref[5, pl.ds(tower, 1), :]
+        ).astype(BF16)
+        pltpu.make_async_copy(out_s.at[slot], out_hbm.at[tower, rows], osem.at[slot]).start()
+        return 0
+
+    lax.fori_loop(0, 8, tile, 0)
+    for c in c2 + last_hop + swaps + own_copy[1:]:
+        c.wait()
+    for i in range(2):
+        pltpu.make_async_copy(out_s.at[i], out_hbm.at[1, 0:256], osem.at[i]).wait()
+    ga = ga_ref.reshape(16, 96, 768)
+    gs = gs_ref.reshape(16, 64, 768)
+    save_ga = pltpu.make_async_copy(ga_ref, ga_hbm, osem.at[2])
+    save_ga.start()
+
+    save_part = pltpu.make_async_copy(q_s.at[:, 0:768], part_hbm, osem.at[3])
+    save_dsp = [
+        pltpu.make_async_copy(kv_s.at[0, 0:768, 0:tokens], dspq_hbm, osem.at[5]),
+        pltpu.make_async_copy(kv_s.at[1, 0:192, 0:tokens], dspp_hbm, osem.at[6]),
+    ]
+    save_uw = pltpu.make_async_copy(x_s.at[0, 0:960], uw_hbm, osem.at[4])
+
+    qv = jnp.concatenate([ga[:, 0:32].reshape(512, 768), gs[:, 0:32].reshape(512, 768)], 0)
+    pv_own = ga[:, 32:48].astype(F32)[:, 8:16].reshape(128, 768)
+    pv_sib = gs[:, 32:48].astype(F32)[:, 8:16].reshape(128, 768)
+    pv = jnp.concatenate([pv_own, pv_sib], 0).astype(BF16)
+    ext_own = ga[:, 48:64].astype(F32)[:, 8:16]
+    ext_sib = gs[:, 48:64].astype(F32)[:, 8:16]
+    _, eq_own = ext_rows(ext_own)
+    _, eq_sib = ext_rows(ext_sib)
+    eq = jnp.concatenate([eq_own, eq_sib], 0)
+    label = (eq[:, 6:7] * 256.0 + eq[:, 7:8]).astype(jnp.int32)
+    col = iota((1, 256), 1)
+    within = lax.rem(col, 128)
+    side = jnp.where(col < 128, g, 1 - g)
+    ids = (within // 8) * 16 + side * 8 + lax.rem(within, 8)
+    logits = SCORE_SCALE * dot_nt(qv, pv)
+    top = jnp.max(logits, -1, keepdims=True)
+    norm_log = top + jnp.log(jnp.sum(jnp.exp(logits - top), -1, keepdims=True))
+    hit = label == ids
+    positive = jnp.sum(jnp.where(hit, logits, 0.0), -1, keepdims=True)
+    grad = (jnp.exp(logits - norm_log) - jnp.where(hit, 1.0, 0.0)).astype(BF16)
+    loss_s[...] = jnp.broadcast_to((norm_log - positive)[:512], (512, 128))
+    own_loss = loss_s[pl.ds(pl.multiple_of(me * 32, 32), 32), 0:32]
+    diagonal = iota((32, 32), 0) == iota((32, 32), 1)
+    loss_ref[...] = jnp.sum(jnp.where(diagonal, own_loss, 0.0), 0, keepdims=True)
+    upq_ref[...] = SCORE_SCALE * dot(grad[:512], pv)
+    upp_ref[...] = SCORE_SCALE * dot_tn(grad[:, 0:128], qv)
+
+    mine = ga[me]
+    low = mine[32:64].astype(F32)
+    gq_rows, keep = [], []
+    for t, (count, up, hidden, vec, q, inn_ref, inv_ref, p_s) in enumerate((
+        (32, upq_ref[pl.ds(pl.multiple_of(me * 32, 32), 32), :], mine[64:96].astype(F32),
+         mine[0:32].astype(F32), qq_ref[...].astype(F32), innq_ref, invq_ref, pq_s),
+        (8, upp_ref[pl.ds(pl.multiple_of(me * 8, 8), 8), :], low[0:8], low[8:16], low[16:24],
+         innp_ref, invp_ref, pp_s),
+    )):
+        g0, g1 = gains_ref[t, 0:1, :], gains_ref[t, 1:2, :]
+        n2 = (vec - biases_ref[5, t:t + 1, :]) / g1
+        n1 = (hidden - biases_ref[3, t:t + 1, :]) / g0
+        grad_second = norm_back(up, g1, n2, inv_ref[:, 1:2])
+        grad_ffn = grad_second.astype(BF16)
+        grad_active = dot_nt(grad_ffn, fout_s[t])
+        _, slope = gelu_pair(inn_ref[...])
+        grad_inner = (grad_active * slope).astype(BF16)
+        grad_hidden = grad_second + dot_nt(grad_inner, fin_s[t])
+        grad_first = norm_back(grad_hidden, g0, n1, inv_ref[:, 0:1])
+        gm = dot_nt(grad_first.astype(BF16), wout_s[t]).astype(BF16)
+        wide = expand_heads(gm.astype(F32)).astype(BF16)
+        dp = dot_nt(wide, kv_s[t, :, 768:1536])
+        soft = p_s[...]
+        ds = (soft * (dp - jnp.sum(soft * dp, -1, keepdims=True))).astype(BF16)
+        gq = fold_heads(dot(ds, kv_s[t, :, 0:768]), count) * KEY_SCALE
+        gq_rows.append(gq)
+        y = dot(ds, x_s[t]) * KEY_SCALE
+        if t == 0:
+            spread = expand_heads(q).astype(BF16)
+            q_s[0, 0:768, :] = dot_tn(y.astype(BF16), spread).astype(BF16)
+            q_s[1, 0:768, :] = dot_tn(zq_ref[...], wide).astype(BF16)
+            save_part.start()
+        else:
+            yt_ref[...] = jnp.concatenate([y, jnp.zeros((32, 768), F32)], 0).T.astype(BF16)
+        at = 768 * t
+        n = HEADS * count
+        u = dot_nt(expand_heads(q).astype(BF16), win_s[t, :, 768:1536]) * KEY_SCALE
+        x_s[0, at:at + n, :] = u.astype(BF16)
+        if t == 0:
+            x_s[0, 384:768, :] = dot_nt(wide, win_s[t, :, 1536:2304]).astype(BF16)
+        else:
+            x_s[0, 864:960, :] = dot_nt(wide, win_s[t, :, 1536:2304]).astype(BF16)
+        kv_s[t, 0:n, 0:tokens] = ds
+        kv_s[t, n:2 * n, 0:tokens] = soft.astype(BF16)
+        save_dsp[t].start()
+        extra = dot_nt(gq.astype(BF16), win_s[t, :, 0:768]) + grad_first
+        ext_ref[32 * t:32 * t + count, :] = extra
+    gq_ref[...] = jnp.concatenate(gq_rows + [jnp.zeros((8, 768), F32)], 0).astype(BF16)
+    save_uw.start()
+    for c in [save_ga, save_part, save_uw] + save_dsp:
+        c.wait()
+
+
+def run_forward(xq, xp, lengths, labels, weights):
+    attn_in, attn_out, ffn_in, ffn_out, gains, biases, ffn_bias = weights
+    tokens = xq.shape[0]
+    vm = pl.BlockSpec(memory_space=pltpu.VMEM)
+    hb = pl.BlockSpec(memory_space=pl.ANY)
+    sds = jax.ShapeDtypeStruct
+    return pl.pallas_call(
+        forward_kernel,
+        out_shape=[
+            sds((2, tokens, 768), BF16), sds((4, 4, 96, 768), BF16), sds((16, 96, 128), BF16),
+            sds((2, 768, 768), BF16), sds((960, 768), BF16),
+            sds((768, tokens), BF16), sds((192, tokens), BF16),
+            sds((1, 32), F32), sds((512, 768), F32), sds((128, 768), F32),
+            sds((48, 768), BF16), sds((768, 128), BF16),
+            sds((40, 768), F32),
+        ],
+        in_specs=[pl.BlockSpec(memory_space=pltpu.SMEM), vm, vm, vm, vm] + [hb] * 6,
+        out_specs=[hb] * 7 + [vm] * 6,
+        scratch_shapes=[
+            pltpu.VMEM((2, tokens, 768), BF16), pltpu.VMEM((2, tokens, 768), BF16),
+            pltpu.VMEM((2, tokens, 1536), BF16),
+            pltpu.VMEM((2, 768, 2304), BF16), pltpu.VMEM((2, 768, 768), BF16),
+            pltpu.VMEM((2, 768, 3072), BF16), pltpu.VMEM((2, 3072, 768), BF16),
+            pltpu.VMEM((384, tokens), F32), pltpu.VMEM((96, tokens), F32),
+            pltpu.VMEM((2, 256, 768), BF16), pltpu.VMEM((256, 768), BF16),
+            pltpu.VMEM((256, 512), F32),
+            pltpu.VMEM((96, 768), BF16), pltpu.VMEM((16, 96, 128), BF16),
+            pltpu.VMEM((4, 4, 96, 768), BF16), pltpu.VMEM((4, 4, 64, 768), BF16),
+            pltpu.VMEM((32, 3072), F32), pltpu.VMEM((8, 3072), F32),
+            pltpu.VMEM((32, 128), F32), pltpu.VMEM((8, 128), F32),
+            pltpu.VMEM((32, 768), BF16), pltpu.VMEM((384, 768), BF16), pltpu.VMEM((512, 128), F32),
+            pltpu.SemaphoreType.DMA((2, 5)), pltpu.SemaphoreType.DMA((2,)), pltpu.SemaphoreType.DMA((7,)),
+            pltpu.SemaphoreType.DMA((15,)), pltpu.SemaphoreType.DMA((15,)),
+            pltpu.SemaphoreType.DMA((16,)), pltpu.SemaphoreType.DMA((16,)),
+        ],
+        compiler_params=pltpu.CompilerParams(
+            collective_id=1, has_side_effects=True, vmem_limit_bytes=63 * 1024 * 1024
+        ),
+        name="forward",
+    )(lengths, labels.reshape(1, -1), gains, biases, ffn_bias, xq, xp, attn_in, attn_out, ffn_in, ffn_out)
+
+
+QR, PR = 512, 128
+
+
+def last_kernel(
+    gains_ref, biases_ref, ffnb_ref, upq_ref, upp_ref, gq_ref, yt_ref,
+    part_hbm, ga_hbm, rsw_hbm, wout_hbm, fin_hbm, fout_hbm,
+    pwin_ref, pwout_ref, pfin_ref, pfout_ref, psum_ref, pffb_ref,
+    swin_ref, swout_ref, sfin_ref, sfout_ref, ssum_ref, sffb_ref,
+    rgq_s, ryt_s, ga_s, rsw_s, own_s, sib_s, r1_s, s2_s, r2_s, wout_s, fin_s, fout_s,
+    act_s, gin_s, gffn_s, gat_s, gm_s, tr_s, acc_s,
+    sem, lsem, ss, rs, as_, ar, xs, xr, ks, kr,
+):
+    me, g = place()
+    greet(me, g)
+    z, yx = me // 4, lax.rem(me, 4)
+    first, second, third = gather_phases(me, g, gq_ref, rgq_s, ss, rs, 0, 0, 48)
+    swaps = []
+    for i in range(1, 16):
+        peer = lax.rem(me + i, 16)
+        swaps.append(remote(yt_ref.at[peer], ryt_s.at[me], as_.at[i], ar.at[i], (peer, g)))
+    own = [
+        pltpu.make_async_copy(gq_ref, rgq_s.at[z, yx], lsem.at[0]),
+        pltpu.make_async_copy(yt_ref.at[me], ryt_s.at[me], lsem.at[1]),
+    ]
+    sib = (me, 1 - g)
+    load_part = pltpu.make_async_copy(part_hbm.at[g], own_s, lsem.at[2])
+    pair = [remote(part_hbm.at[1 - g], sib_s, ks.at[0], kr.at[0], sib)]
+    xpeer = me + 1 - 2 * lax.rem(me, 2)
+    ypeer = me + 2 - 4 * (lax.rem(me, 4) // 2)
+    dpeer = xpeer + 2 - 4 * (lax.rem(xpeer, 4) // 2)
+    plane = [
+        remote(own_s.at[:, lax.rem(peer, 4)], r1_s.at[k], ks.at[1 + k], kr.at[1 + k], (peer, g))
+        for k, peer in enumerate((dpeer, xpeer, ypeer))
+    ]
+    column = [
+        remote(s2_s.at[lax.rem(z + d, 4)], r2_s.at[d - 1], ks.at[3 + d], kr.at[3 + d],
+               (lax.rem(z + d, 4) * 4 + yx, g))
+        for d in range(1, 4)
+    ]
+
+    def add_pair():
+        def one(i, _):
+            own_s[i] = (own_s[i].astype(F32) + sib_s[i].astype(F32)).astype(BF16)
+            return 0
+
+        lax.fori_loop(0, 4, one, 0)
+
+    def add_plane():
+        def one(i, _):
+            s2_s[i] = (
+                own_s[i, yx].astype(F32) + r1_s[0, i].astype(F32)
+                + r1_s[1, i].astype(F32) + r1_s[2, i].astype(F32)
+            ).astype(BF16)
+            return 0
+
+        lax.fori_loop(0, 4, one, 0)
+
+    early = [
+        remote(pwout_ref, swout_ref, xs.at[0], xr.at[0], sib),
+        remote(pfin_ref, sfin_ref, xs.at[1], xr.at[1], sib),
+        remote(pfout_ref, sfout_ref, xs.at[2], xr.at[2], sib),
+        remote(pffb_ref, sffb_ref, xs.at[3], xr.at[3], sib),
+    ]
+    late = [
+        remote(pwin_ref, swin_ref, xs.at[4], xr.at[4], sib),
+        remote(psum_ref, ssum_ref, xs.at[5], xr.at[5], sib),
+    ]
+    load_ga = pltpu.make_async_copy(ga_hbm, ga_s, sem.at[0])
+    load_fin = [pltpu.make_async_copy(fin_hbm.at[t], fin_s.at[t], sem.at[1 + t]) for t in range(2)]
+    load_fout = [pltpu.make_async_copy(fout_hbm.at[t], fout_s.at[t], sem.at[3 + t]) for t in range(2)]
+    load_wout = pltpu.make_async_copy(wout_hbm, wout_s, sem.at[5])
+    load_rest = [
+        pltpu.make_async_copy(rsw_hbm, rsw_s, sem.at[6]),
+    ]
+    for c in [load_part, load_ga, load_fin[0], load_fout[0], load_wout, load_fin[1], load_fout[1]] + load_rest + own:
+        c.start()
+    greeted()
+    for c in pair + first + swaps:
+        c.start()
+
+    load_ga.wait()
+    load_wout.wait()
+    ext = ga_s[:, 48:64].astype(F32)[:, 8:16]
+    ext_p, ext_q = ext_rows(ext)
+    psum_ref[...] = jnp.zeros(psum_ref.shape, F32)
+    pffb_ref[...] = jnp.zeros(pffb_ref.shape, F32)
+
+    def chain(t, up, hidden, vec, inv1, inv2, rows, count):
+        g0, g1 = gains_ref[t, 0:1, :], gains_ref[t, 1:2, :]
+        n2 = (vec.astype(F32) - biases_ref[5, t:t + 1, :]) / g1
+        n1 = (hidden.astype(F32) - biases_ref[3, t:t + 1, :]) / g0
+        grad_second = norm_back(up, g1, n2, inv2)
+        grad_ffn = grad_second.astype(BF16)
+        gffn_s[rows, :] = grad_ffn
+        grad_hidden = grad_second
+        for c in range(4):
+            cols = slice(768 * c, 768 * c + 768)
+            inner = dot(hidden, fin_s[t, :, cols]) + ffnb_ref[t:t + 1, cols]
+            active, slope = gelu_pair(inner)
+            act_s[rows, cols] = active.astype(BF16)
+            grad_inner = (dot_nt(grad_ffn, fout_s[t, cols, :]) * slope).astype(BF16)
+            gin_s[rows, cols] = grad_inner
+            pffb_ref[t:t + 1, cols] += jnp.sum(grad_inner.astype(F32), 0, keepdims=True)
+            grad_hidden = grad_hidden + dot_nt(grad_inner, fin_s[t, :, cols])
+        grad_first = norm_back(grad_hidden, g0, n1, inv1)
+        grad_attn = grad_first.astype(BF16)
+        gat_s[rows, :] = grad_attn
+        gm = dot_nt(grad_attn, wout_s[t]).astype(BF16)
+        gm_s[rows, :] = gm
+        total = lambda v: jnp.sum(v, 0, keepdims=True)
+        psum_ref[t, 0:8, :] += jnp.concatenate([
+            total(grad_hidden * n1), total(up * n2), jnp.zeros((1, 768), F32),
+            total(gm.astype(F32)), total(grad_attn.astype(F32)), total(grad_hidden),
+            total(grad_ffn.astype(F32)), total(up),
+        ], 0)
+
+    i1q, i2q = decode_inv(ext_q)
+    i1p, i2p = decode_inv(ext_p)
+    for blk in range(2):
+        if blk == 0:
+            load_fin[0].wait()
+            load_fout[0].wait()
+        lo = blk * 256
+        chain(
+            0, upq_ref[lo:lo + 256, :],
+            ga_s[8 * blk:8 * blk + 8, 64:96].reshape(256, 768),
+            ga_s[8 * blk:8 * blk + 8, 0:32].reshape(256, 768),
+            i1q[lo:lo + 256], i2q[lo:lo + 256], slice(lo, lo + 256), 256,
+        )
+        if blk == 0:
+            load_part.wait()
+            for c in pair:
+                c.wait()
+            add_pair()
+            for c in plane:
+                c.start()
+            own[0].wait()
+            for c in first:
+                c.wait()
+            for c in second:
+                c.start()
+    load_fin[1].wait()
+    load_fout[1].wait()
+    hv = ga_s[:, 32:48].astype(F32)
+    chain(
+        1, upp_ref[...], hv[:, 0:8].reshape(128, 768).astype(BF16),
+        hv[:, 8:16].reshape(128, 768).astype(BF16), i1p, i2p, slice(QR, QR + PR), 128,
+    )
+    for c in plane:
+        c.wait()
+    add_plane()
+    for c in column:
+        c.start()
+    for c in second:
+        c.wait()
+    for c in third:
+        c.start()
+
+    for c in load_rest:
+        c.wait()
+    for t, rows in enumerate((slice(0, QR), slice(QR, QR + PR))):
+        count = rows.stop - rows.start
+        fo_at = pl.multiple_of((me // 2) * 384, 128)
+        tr_s[:, 0:count] = act_s[rows, pl.ds(fo_at, 384)].astype(F32).T.astype(BF16)
+        fo_row = pl.multiple_of(lax.rem(me, 2) * 192, 16)
+        pfout_ref[t] = dot(tr_s[pl.ds(fo_row, 192), 0:count], gffn_s[rows, :])
+        fi_at = pl.multiple_of((me // 8) * 384, 128)
+        if t == 0:
+            hid = ga_s[:, 64:96, pl.ds(fi_at, 384)].reshape(QR, 384)
+        else:
+            hid = ga_s[:, 32:48, pl.ds(fi_at, 384)].astype(F32)[:, 0:8].reshape(PR, 384)
+        tr_s[:, 0:count] = hid.astype(F32).T.astype(BF16)
+        fi_row = pl.multiple_of(lax.rem(me, 8) * 48, 16)
+        pfin_ref[t] = dot(tr_s[pl.ds(fi_row, 48), 0:count], gin_s[rows, :])
+        if t == 0:
+            mx = rsw_s[:, 0:32].reshape(QR, 128)
+        else:
+            mx = rsw_s[:, 32:48].astype(F32)[:, 0:8].reshape(PR, 128).astype(BF16)
+        pwout_ref[t] = dot_tn(mx, gat_s[rows, :])[0:48]
+    for c in early:
+        c.start()
+
+    def low_rank(read_t, read_p, out_col):
+        acc_s[...] = jnp.zeros(acc_s.shape, F32)
+
+        def source(i, _):
+            wide = jnp.concatenate([expand_heads(read_p(i)), jnp.zeros((32, 768), F32)], 0)
+            acc_s[...] += dot(read_t(i), wide.astype(BF16))
+            return 0
+
+        lax.fori_loop(0, 16, source, 0)
+        pwin_ref[1, :, out_col:out_col + 768] = acc_s[...]
+
+    def gm_p(i):
+        pair = gm_s[pl.ds(pl.multiple_of(QR + (i // 2) * 16, 16), 16), :].astype(F32)
+        return jnp.where(lax.rem(i, 2) == 0, pair[0:8], pair[8:16])
+
+    low_rank(lambda i: rsw_s[i, 48:96, :], gm_p, 1536)
+
+    for c in third:
+        c.wait()
+    for c in swaps:
+        c.wait()
+    own[1].wait()
+
+    def q_p(i):
+        return ga_s[i, 48:64, :].astype(F32)[0:8]
+
+    low_rank(lambda i: ryt_s[i], q_p, 768)
+    rg_q = rgq_s[:, :, 0:32].reshape(QR, 768)
+    rg_p = rgq_s[:, :, 32:48].astype(F32)[:, :, 0:8].reshape(PR, 768)
+    pwin_ref[0, :, 0:768] = dot_tn(rsw_s[:, 0:32].reshape(QR, 128), rg_q)[64:112]
+    x_p = rsw_s[:, 32:48].astype(F32)[:, 0:8].reshape(PR, 128).astype(BF16)
+    pwin_ref[1, :, 0:768] = dot_tn(x_p, rg_p.astype(BF16))[64:112]
+    for c in column:
+        c.wait()
+    pwin_ref[0, :, pl.ds(pl.multiple_of(768 + 768 * g, 128), 768)] = (
+        s2_s[z].astype(F32) + r2_s[0].astype(F32) + r2_s[1].astype(F32) + r2_s[2].astype(F32)
+    )
+    pwin_ref[0, :, pl.ds(pl.multiple_of(1536 - 768 * g, 128), 768)] = jnp.zeros((48, 768), F32)
+    psum_ref[0, 2:3, :] = jnp.sum(rg_q.astype(F32), 0, keepdims=True)
+    psum_ref[1, 2:3, :] = jnp.sum(rg_p, 0, keepdims=True)
+    for c in late:
+        c.start()
+    for c in early + late:
+        c.wait()
+
+
+def last(weights, upq, upp, gq, yt, part, ga, rsw):
+    attn_in, attn_out, ffn_in, ffn_out, gains, biases, ffn_bias = weights
+    vm = pl.BlockSpec(memory_space=pltpu.VMEM)
+    hb = pl.BlockSpec(memory_space=pl.ANY)
+    sds = jax.ShapeDtypeStruct
+    parts = [
+        sds((2, 48, 2304), F32), sds((2, 48, 768), F32), sds((2, 48, 3072), F32),
+        sds((2, 192, 768), F32), sds((2, 8, 768), F32), sds((2, 3072), F32),
+    ]
+    return pl.pallas_call(
+        last_kernel,
+        out_shape=parts + parts,
+        in_specs=[vm] * 7 + [hb] * 6,
+        out_specs=[vm] * 12,
+        scratch_shapes=[
+            pltpu.VMEM((4, 4, 48, 768), BF16), pltpu.VMEM((16, 48, 128), BF16),
+            pltpu.VMEM((16, 96, 768), BF16), pltpu.VMEM((16, 96, 128), BF16),
+            pltpu.VMEM((4, 4, 48, 768), BF16), pltpu.VMEM((4, 4, 48, 768), BF16),
+            pltpu.VMEM((3, 4, 48, 768), BF16), pltpu.VMEM((4, 48, 768), BF16),
+            pltpu.VMEM((3, 48, 768), BF16), pltpu.VMEM((2, 768, 768), BF16),
+            pltpu.VMEM((2, 768, 3072), BF16), pltpu.VMEM((2, 3072, 768), BF16),
+            pltpu.VMEM((640, 3072), BF16), pltpu.VMEM((640, 3072), BF16),
+            pltpu.VMEM((640, 768), BF16), pltpu.VMEM((640, 768), BF16), pltpu.VMEM((640, 768), BF16),
+            pltpu.VMEM((384, 512), BF16),
+            pltpu.VMEM((48, 768), F32),
+            pltpu.SemaphoreType.DMA((11,)), pltpu.SemaphoreType.DMA((4,)),
+            pltpu.SemaphoreType.DMA((7,)), pltpu.SemaphoreType.DMA((7,)),
+            pltpu.SemaphoreType.DMA((16,)), pltpu.SemaphoreType.DMA((16,)),
+            pltpu.SemaphoreType.DMA((6,)), pltpu.SemaphoreType.DMA((6,)),
+            pltpu.SemaphoreType.DMA((7,)), pltpu.SemaphoreType.DMA((7,)),
+        ],
+        compiler_params=pltpu.CompilerParams(
+            collective_id=2, has_side_effects=True, vmem_limit_bytes=62 * 1024 * 1024
+        ),
+        name="last",
+    )(gains, biases, ffn_bias, upq, upp, gq, yt.reshape(16, 48, 128),
+      part.reshape(2, 4, 4, 48, 768), ga.reshape(16, 96, 768), rsw, attn_out, ffn_in, ffn_out)
+
+
+def finish_kernel(
+    lens_ref, loss_in, ext_ref, dspq_hbm, dspp_hbm, uw_hbm, raw_hbm, *refs,
+):
+    ins, outs, (loss_ref, outq_hbm, outp_hbm, dxq_hbm, dxp_hbm), scratch = (
+        refs[:12], refs[12:19], refs[19:24], refs[24:]
+    )
+    part_s, raw_s, sum_s = scratch[:12], scratch[12], scratch[13:17]
+    dx_s, dspq_ref, dspp_ref, uw_ref, psem, rsem, ssem, dsem, osem = scratch[17:]
+    me, _ = place()
+    raw_in = pltpu.make_async_copy(raw_hbm, raw_s, rsem.at[2])
+    raw_out = [pltpu.make_async_copy(raw_s.at[t], (outq_hbm, outp_hbm)[t], rsem.at[t]) for t in range(2)]
+    gets = [
+        pltpu.make_async_copy(uw_hbm, uw_ref, osem.at[0]),
+        pltpu.make_async_copy(dspq_hbm, dspq_ref, osem.at[1]),
+        pltpu.make_async_copy(dspp_hbm, dspp_ref, osem.at[2]),
+    ]
+    for c in gets:
+        c.start()
+    raw_in.start()
+    loads = [pltpu.make_async_copy(ins[k], part_s[k], psem.at[k]) for k in range(12)]
+    for c in loads:
+        c.start()
+    loss_ref[...] = loss_in[...]
+
+    for c in gets:
+        c.wait()
+    extra_p = ext_ref[32:40, :]
+    e_hi = extra_p.astype(BF16).astype(F32)
+    uw_p = jnp.concatenate([uw_ref[768:960, :].astype(F32), e_hi, extra_p - e_hi], 0).astype(BF16)
+    keep = []
+    for t in range(2):
+        for m in range(4):
+            cols = slice(256 * m, 256 * m + 256)
+            k = t * 4 + m
+            if k >= 2:
+                keep[k - 2].wait()
+            if t == 0:
+                dx_s[k % 2] = dot_tn(dspq_ref[:, cols], uw_ref[0:768, :])
+                for c in range(8):
+                    dx_s[k % 2, 32 * c:32 * c + 1, :] += ext_ref[8 * m + c:8 * m + c + 1, :]
+            else:
+                colr = iota((8, 256), 1) + 256 * m
+                rowr = iota((8, 256), 0)
+                start = jnp.zeros((8, 256), jnp.int32)
+                for r in range(2):
+                    at = jnp.int32(r * 512)
+                    for c in range(4):
+                        start = jnp.where(rowr == r * 4 + c, at, start)
+                        at = at + lens_ref[r, c]
+                sel = jnp.where(colr == start, 1.0, 0.0)
+                sel2 = jnp.concatenate([sel, sel], 0).astype(BF16)
+                lhs = jnp.concatenate([dspp_ref[:, cols], sel2], 0)
+                dx_s[k % 2] = dot_tn(lhs, uw_p)
+            c = pltpu.make_async_copy(dx_s.at[k % 2], (dxq_hbm, dxp_hbm)[t].at[cols], dsem.at[k % 2])
+            c.start()
+            keep.append(c)
+            if k == 1:
+                raw_in.wait()
+                for c in raw_out:
+                    c.start()
+
+    stores = []
+    for k in range(4):
+        loads[k].wait()
+        loads[6 + k].wait()
+        sum_s[k][...] = part_s[k][...] + part_s[6 + k][...]
+        c = pltpu.make_async_copy(sum_s[k], outs[k], ssem.at[k])
+        c.start()
+        stores.append(c)
+    for k in (4, 5, 10, 11):
+        loads[k].wait()
+    shift = lax.rem(768 - 48 * me, 768)
+    for t in range(2):
+        sums = pltpu.roll(part_s[4][t] + part_s[10][t], shift, 1)[:, 0:48]
+        outs[4][t] = sums[0:2]
+        for j in range(6):
+            outs[5][j, t:t + 1, :] = sums[2 + j:3 + j]
+    ffb = part_s[5][...] + part_s[11][...]
+    wide = jnp.concatenate([ffb, jnp.zeros((6, 3072), F32)], 0)
+    outs[6][...] = pltpu.roll(wide, lax.rem(3072 - 192 * me, 3072), 1)[0:2, 0:192]
+    for c in keep[6:] + stores + raw_out:
+        c.wait()
+
+
+def finish(lengths, loss, dspq, dspp, uw, ext, raw, parts):
+    sds = jax.ShapeDtypeStruct
+    tokens = dspq.shape[1]
+    vm = pl.BlockSpec(memory_space=pltpu.VMEM)
+    hb = pl.BlockSpec(memory_space=pl.ANY)
+    return pl.pallas_call(
+        finish_kernel,
+        out_shape=[sds(p.shape, F32) for p in parts[:4]]
+        + [sds((2, 2, 48), F32), sds((6, 2, 48), F32), sds((2, 192), F32)]
+        + [sds((1, 32), F32), sds((tokens, 768), BF16), sds((tokens, 768), BF16)]
+        + [sds((tokens, 768), F32), sds((tokens, 768), F32)],
+        in_specs=[pl.BlockSpec(memory_space=pltpu.SMEM)] + [vm] * 2 + [hb] * 16,
+        out_specs=[hb] * 4 + [vm] * 4 + [hb] * 4,
+        scratch_shapes=[pltpu.VMEM(p.shape, F32) for p in parts]
+        + [pltpu.VMEM((2, tokens, 768), BF16)]
+        + [pltpu.VMEM(p.shape, F32) for p in parts[:4]]
+        + [pltpu.VMEM((2, 256, 768), F32), pltpu.VMEM((768, tokens), BF16)]
+        + [pltpu.VMEM((192, tokens), BF16), pltpu.VMEM((960, 768), BF16)]
+        + [pltpu.SemaphoreType.DMA((n,)) for n in (12, 3, 4, 2, 3)],
+        compiler_params=pltpu.CompilerParams(vmem_limit_bytes=VMEM_LIMIT),
+        name="finish",
+    )(lengths, loss, ext, dspq, dspp, uw, raw, *parts)
+
+
+def fast_shards(query_tokens, passage_tokens, lengths, labels, *weights):
+    xq = query_tokens.reshape(-1, 768)
+    xp = passage_tokens.reshape(-1, 768)
+    weights = weights[:5] + (weights[5].transpose(1, 0, 2), weights[6])
+    raw, ga, rsw, part, uw, dspq, dspp, loss, upq, upp, gq, yt, ext = run_forward(
+        xq, xp, lengths, labels, weights
+    )
+    parts = last(weights, upq, upp, gq, yt, part, ga, rsw)
+    win, wout, fin, fout, gains, biases, ffb, loss, outq, outp, dxq, dxp = finish(
+        lengths, loss, dspq, dspp, uw, ext, raw, parts
+    )
+    return (
+        loss.reshape(-1),
+        outq.reshape(query_tokens.shape),
+        outp.reshape(passage_tokens.shape),
+        dxq.reshape(query_tokens.shape),
+        dxp.reshape(passage_tokens.shape),
+        win, wout, fin, fout, gains, biases.transpose(1, 0, 2), ffb,
+    )
 
 
 def layer_norm(residual, gain_vec, shift_vec):
@@ -17,7 +913,7 @@
     return centre * inverse * gain_vec + shift_vec
 
 
-def norm_back(residual, gain_vec, upstream):
+def plain_norm_back(residual, gain_vec, upstream):
     centre = residual - jnp.mean(residual, -1, keepdims=True)
     inverse = lax.rsqrt(jnp.mean(centre * centre, -1, keepdims=True) + EPSILON)
     normed = centre * inverse
@@ -89,14 +985,14 @@
     per_row = starts.shape[1]
     feature = flat_tokens.shape[1]
     head_count = feature // HEAD_DIM
-    grad_second, gain_two, shift_two = norm_back(second_cls, gains[1], upstream)
+    grad_second, gain_two, shift_two = plain_norm_back(second_cls, gains[1], upstream)
     grad_ffn = grad_second.astype(jnp.bfloat16)
     grad_down = jnp.dot(active_cls.T, grad_ffn, preferred_element_type=jnp.float32)
     grad_active = jnp.dot(grad_ffn, ffn_out.T, preferred_element_type=jnp.float32)
     grad_inner = jax.vjp(jax.nn.gelu, inner_cls)[1](grad_active)[0].astype(jnp.bfloat16)
     grad_up = jnp.dot(hidden_cls.T, grad_inner, preferred_element_type=jnp.float32)
     grad_hidden = grad_second + jnp.dot(grad_inner, ffn_in.T, preferred_element_type=jnp.float32)
-    grad_first, gain_one, shift_one = norm_back(first_cls, gains[0], grad_hidden)
+    grad_first, gain_one, shift_one = plain_norm_back(first_cls, gains[0], grad_hidden)
     grad_attn = grad_first.astype(jnp.bfloat16)
     grad_outproj = jnp.dot(mixed_cls.T, grad_attn, preferred_element_type=jnp.float32)
     grad_mixed = jnp.dot(grad_attn, attn_out.T, preferred_element_type=jnp.float32).astype(
@@ -309,8 +1205,9 @@
         P(),
         P(),
     )
+    small = dict(mesh.shape) == {"blk": 16, "grp": 2}
     return jax.shard_map(
-        shards,
+        fast_shards if small else shards,
         mesh=mesh,
         in_specs=placed,
         out_specs=(

time: 1680 us -> 169 us (0.10)
  waiting for transfers between devices: 1020 us -> 0 us
  local copies, waits for them, and re-layouts: 275 us -> 0 us
  matrix products: 183 us -> 0 us
  Pallas kernels: 0 us -> 165 us
  other arithmetic: 92.2 us -> 0 us
  blocking collectives: 88 us -> 0 us
    unnamed x13 -> x0, waiting for transfers between devices: 518 us -> none
    reduce_scatter x3 -> x0, waiting for transfers between devices: 481 us -> none  [the longest x1 176 us: shards(): lax.psum_scatter(grad_down.astype(jnp.bfloat16), 'blk', scatter_dimension...]
    dot_general x39 -> x0, matrix products: 168 us -> none  [the longest x2 25.1 us: forward(): jnp.dot(hidden, ffn_in, preferred_element_type=jnp.float32) + ffn_bias]
    pallas_call x0 -> x3, Pallas kernels: none -> 165 us  [the longest x1 93.6 us: run_forward(): pl.pallas_call(forward_kernel, out_shape=[sds((2, tokens, 768), BF16), sd...]
    gather x177 -> x0, local copies, waits for them, and re-layouts: 149 us -> none
    unnamed x1 -> x0, blocking collectives: 51 us -> none
    reshape x6 -> x0, local copies, waits for them, and re-layouts: 40.6 us -> none  [the longest x2 23.9 us: forward(): shaped = joined.reshape(batch_size, seq_len, 3, head_count, HEAD_DIM)]
    another operation x20 -> x0, other arithmetic: 39.1 us -> none  [the longest x9 22.1 us: shards(): jnp.stack([first_part, second_part])]
  transfers between devices with their start and end apart: 9 -> 0, of which waited for: 8 -> 0; matrix products, arithmetic and copies ran while one was open for 23% -> 0% of each run, Pallas kernels for 0% -> 0%
where the time goes in v1:
time: 169 us; the launch traced here: 166 us
  Pallas kernels  165 us (98%)
    pallas_call x1, Pallas kernels, run_forward(): pl.pallas_call(forward_kernel, out_shape=[sds((2, tokens, 768), BF16), sd...  93.6 us
    pallas_call x1, Pallas kernels, last(): pl.pallas_call(last_kernel, out_shape=parts + parts, in_specs=[vm] * 7 +...  58.6 us
    pallas_call x1, Pallas kernels, finish(): pl.pallas_call(finish_kernel, out_shape=[sds(p.shape, F32) for p in parts...  12.9 us

profile of v1, /device:TPU:9, one launch (start us, length us, event | category | flops | bytes accessed | tf_op | source)
XLA Modules:
  0.0 166.0 jit_solution(8217949784860219795)
XLA Ops:
  0.6 93.6 %forward.1 = (bf16[2,1024,768]{2,1,0:T(8,128)(2,1)}, bf16[4,4,96,768]{3,2,1,0:T(8,128)(2,1)}, bf16[16,96,128]{2,1,0:T(8,128)(2,1)}, bf16[2,768,768]{2,1,0:T(8,12...) custom-call(s32[2,4]{1,0:T(2,128)} %lens_ref.3, ...), custom_call_target="tpu_custom_call" | custom-call | tf_op jit(solution)/shard_map/forward/pallas_call | solution.py:478
  94.2 58.6 %last.1 = (f32[2,48,2304]{2,1,0:T(8,128)}, f32[2,48,768]{2,1,0:T(8,128)}, f32[2,48,3072]{2,1,0:T(8,128)}, f32[2,192,768]{2,1,0:T(8,128)}, f32[2,8,768]{2,1,0:T(8...) custom-call(f32[2,2,768]{2,1,0:T(2,128)} %gains_ref.3, ...), custom_call_target="tpu_custom_call" | custom-call | tf_op jit(solution)/shard_map/last/pallas_call | solution.py:751
  152.9 12.9 %finish.1 = (f32[2,48,2304]{2,1,0:T(8,128)}, f32[2,48,768]{2,1,0:T(8,128)}, f32[2,48,3072]{2,1,0:T(8,128)}, f32[2,192,768]{2,1,0:T(8,128)}, f32[2,2,48]{2,1,0:T(...) custom-call(s32[2,4]{1,0:T(2,128)} %lens_ref.3, ...), custom_call_target="tpu_custom_call" | custom-call | tf_op jit(solution)/shard_map/finish/pallas_call | solution.py:870
